TPU v7x, 128 devices: a whole 4x4x4 slice. The times are simulated.
128 devices in a mesh: dom: 8 (over z, core), grp: 16 (over x, y).
Axes of the slice: x: 4, y: 4, z: 4, core: 2. Of those that a mesh axis runs over, the one named last changes fastest.
Arguments:
- inputs: bfloat16 [393216, 256], P(('dom', 'grp')), may hold values from -6 to 6
- initial: bfloat16 [393216, 256], P(('dom', 'grp')), may hold values from -6 to 6
- history: bfloat16 [393216, 256], P(('dom', 'grp')), may hold values from -6 to 6
- upstream: bfloat16 [393216, 256], P(('dom', 'grp')), may hold values from -6 to 6
- weight: bfloat16 [256, 256], replicated, may hold values from -0.375 to 0.375
- tile_vals: bfloat16 [36864, 128, 128], P(('dom', 'grp')), may hold values from 0 to 0.088378906
- tile_row: int32 [36864], P(('dom', 'grp')), may hold values from 0 to 23
- tile_col: int32 [36864], P(('dom', 'grp')), may hold values from 0 to 47, as said below
- tile_count: int32 [128], P(('dom', 'grp')), may hold values from 48 to 288, as said below
- send_rows: int32 [8, 16, 128, 8], P('dom', 'grp'), may hold values from 0 to 3071
- cache_ask: int32 [8, 16, 8, 2], P('dom', 'grp'), may hold values from 0 to 23
Outputs:
- layer_out: bfloat16 [393216, 256], P(('dom', 'grp'))
- grad_inputs: float32 [393216, 256], P(('dom', 'grp'))
- grad_weight: float32 [256, 256], replicated
Inputs may be any that keep to these rules, and one draw needn't show every extreme that they name: `send_rows`: row numbers within the sending section. `cache_ask`: block numbers within the owning section. `tile_row`: row block within the section. `tile_col`: in each section's list the first 48 tiles name every column block once. `tile_count`: some section has exactly 288 live tiles.
All inputs are finite; a program needn't handle non-finite values.
Results may differ from a plain program's by a relative error of at most 0.0053.
Values may be sent and summed in bfloat16 or wider, within the bound.
A program may use at most 128 MiB of HBM per device.

v0:
```python
import math
import jax
import jax.numpy as jnp
from jax import lax
from jax.sharding import PartitionSpec as P

alpha_res = 0.1
beta_map = 0.4


def silu_slope(pre_act):
    squash = jax.nn.sigmoid(pre_act)
    return squash * (1.0 + pre_act * (1.0 - squash))


def turn_width(slot_count):
    for option_width in (96, 48, 32, 16, 8):
        return option_width
    return slot_count


def per_device(
    inputs,
    initial,
    history,
    upstream,
    weight,
    tile_vals,
    tile_row,
    tile_col,
    tile_count,
    send_rows,
    cache_ask,
):
    row_count, feature_dim = inputs.shape
    block_rows = tile_vals.shape[1]
    block_count = row_count // block_rows
    slot_count = tile_vals.shape[0]
    group_size = turn_width(slot_count)
    dom_count = lax.axis_size("dom")
    grp_count = lax.axis_size("grp")
    peer_count = dom_count * grp_count
    send_list = send_rows.reshape(peer_count, -1)
    per_peer = send_list.shape[1]
    ask_list = cache_ask.reshape(dom_count, -1)
    asked_per = ask_list.shape[1]
    outgoing = inputs[send_list.reshape(-1)].reshape(peer_count, per_peer, feature_dim)
    arrived = lax.all_to_all(outgoing, ("dom", "grp"), split_axis=0, concat_axis=0, tiled=True)
    arrived = arrived.reshape(peer_count * per_peer, feature_dim)
    wanted = lax.all_to_all(ask_list, "dom", split_axis=0, concat_axis=0, tiled=True)
    own_blocks = history.reshape(block_count, block_rows, feature_dim)
    served = own_blocks[wanted.reshape(-1)].reshape(dom_count, asked_per * block_rows, feature_dim)
    cached = lax.all_to_all(served, "dom", split_axis=0, concat_axis=0, tiled=True)
    cached = cached.reshape(dom_count * asked_per * block_rows, feature_dim)
    columns = jnp.concatenate([inputs, arrived, cached], axis=0)
    col_blocks = columns.reshape(-1, block_rows, feature_dim)
    column_total = col_blocks.shape[0]
    live_count = tile_count[0]
    turn_count = (live_count + group_size - 1) // group_size

    def turn_slices(turn_index):
        offset = turn_index * group_size
        tile_block = lax.dynamic_slice_in_dim(tile_vals, offset, group_size, 0)
        row_pick = lax.dynamic_slice_in_dim(tile_row, offset, group_size, 0)
        col_pick = lax.dynamic_slice_in_dim(tile_col, offset, group_size, 0)
        live_part = (offset + jnp.arange(group_size) < live_count).astype(jnp.float32)
        return (tile_block, row_pick, col_pick, live_part)

    def forward_turn(turn_index, totals):
        tile_block, row_pick, col_pick, live_part = turn_slices(turn_index)
        products = jnp.einsum(
            "tij,tjd->tid", tile_block, col_blocks[col_pick], preferred_element_type=jnp.float32
        )
        placing = (row_pick[:, None] == jnp.arange(block_count)[None, :]).astype(
            jnp.float32
        ) * live_part[:, None]
        return totals + jnp.einsum(
            "tr,tid->rid", placing, products, precision=lax.Precision.HIGHEST
        )

    gathered = lax.fori_loop(
        0, turn_count, forward_turn, jnp.zeros((block_count, block_rows, feature_dim), jnp.float32)
    )
    mixture = (1.0 - alpha_res) * gathered.reshape(
        row_count, feature_dim
    ) + alpha_res * initial.astype(jnp.float32)
    mixed_b = mixture.astype(jnp.bfloat16)
    pre_act = (1.0 - beta_map) * mixture + beta_map * jnp.dot(
        mixed_b, weight, preferred_element_type=jnp.float32
    )
    layer_out = jax.nn.silu(pre_act).astype(jnp.bfloat16)
    act_slope = upstream.astype(jnp.float32) * silu_slope(pre_act)
    slope_b = act_slope.astype(jnp.bfloat16)
    weight_part = lax.dot_general(
        mixed_b, slope_b, (((0,), (0,)), ((), ())), preferred_element_type=jnp.float32
    )
    through_weight = lax.dot_general(
        slope_b, weight, (((1,), (1,)), ((), ())), preferred_element_type=jnp.float32
    )
    back_grad = (
        (1.0 - alpha_res) * ((1.0 - beta_map) * act_slope + beta_map * through_weight)
    ).astype(jnp.bfloat16)
    back_blocks = back_grad.reshape(block_count, block_rows, feature_dim)

    def backward_turn(turn_index, totals):
        tile_block, row_pick, col_pick, live_part = turn_slices(turn_index)
        spread = jnp.einsum(
            "tji,tjd->tid", tile_block, back_blocks[row_pick], preferred_element_type=jnp.float32
        )
        onto_mask = (col_pick[:, None] == jnp.arange(column_total)[None, :]).astype(
            jnp.float32
        ) * live_part[:, None]
        return totals + jnp.einsum(
            "tc,tid->cid", onto_mask, spread, precision=lax.Precision.HIGHEST
        )

    column_grads = lax.fori_loop(
        0,
        turn_count,
        backward_turn,
        jnp.zeros((column_total, block_rows, feature_dim), jnp.float32),
    )
    fresh_blocks = peer_count * per_peer // block_rows
    own_grads = column_grads[:block_count].reshape(row_count, feature_dim)
    fresh_grads = (
        column_grads[block_count : block_count + fresh_blocks]
        .reshape(peer_count, per_peer, feature_dim)
        .astype(jnp.bfloat16)
    )
    returned = lax.all_to_all(fresh_grads, ("dom", "grp"), split_axis=0, concat_axis=0, tiled=True)
    returned = returned.reshape(peer_count * per_peer, feature_dim).astype(jnp.float32)
    grad_inputs = own_grads.at[send_list.reshape(-1)].add(returned)
    weight_total = lax.psum(weight_part, ("dom", "grp"))
    grad_weight = weight_total * (beta_map / math.sqrt(row_count * peer_count))
    return (layer_out, grad_inputs, grad_weight)


def solution(mesh):
    placed = (
        P(("dom", "grp"), None),
        P(("dom", "grp"), None),
        P(("dom", "grp"), None),
        P(("dom", "grp"), None),
        P(),
        P(("dom", "grp"), None, None),
        P(("dom", "grp")),
        P(("dom", "grp")),
        P(("dom", "grp")),
        P("dom", "grp", None, None),
        P("dom", "grp", None, None),
    )
    return jax.shard_map(
        per_device,
        mesh=mesh,
        in_specs=placed,
        out_specs=(P(("dom", "grp"), None), P(("dom", "grp"), None), P()),
        check_vma=False,
    )
```

profile of v0, /device:TPU:1, one launch (start us, length us, event | category | flops | bytes accessed | tf_op | source)
XLA Modules:
  0.0 450.1 jit_solution(1641534458222594287)
XLA Ops:
  7.2 1.5 copy.25
  8.6 6.8 %all-to-all-start.1 = ((s32[8,1,2]{2,1,0:T(1,128)}), s32[8,1,2]{2,1,0:T(1,128)S(1)}, u32[]{:S(2)}, u32[]{:S(2)}) async-start(s32[8,1,2]{2,1,0:T(1,128)} %copy.25), calls=%async_computation.1 | async-start | bytes 8192 | tf_op jit(solution)/shard_map/all_to_all | solution.py:50
  15.5 0.8 copy.24
  16.2 0.1 reshape_reshape.4
  16.4 0.6 copy-done.9
  17.0 6.2 %gather_fusion.2 = bf16[1024,256]{1,0:T(8,128)(2,1)} fusion(bf16[3072,256]{1,0:T(8,128)(2,1)} %param.15, s32[1024]{0:T(1024)S(1)} %broadcast_clamp_fusion), kind=kCustom, calls=%fused_computation.2 | custom fusion | bytes 1052672 | tf_op jit(solution)/shard_map/gather | solution.py:47
  23.2 9.9 %all-to-all-start = ((bf16[128,8,256]{2,1,0:T(8,128)(2,1)}), bf16[128,8,256]{2,1,0:T(8,128)(2,1)}, u32[]{:S(2)}, u32[]{:S(2)}) async-start(bf16[128,8,256]{2,1,0:T(8,128)(2,1)} %bitcast.49), calls=%async_computation | async-start | bytes 1048576 | tf_op jit(solution)/shard_map/all_to_all | solution.py:48
  33.1 0.5 broadcast.141
  33.6 0.7 reduce.3
  34.3 0.1 reshape.119
  34.4 1.6 gather_fusion.3
  36.0 10.1 %all-to-all-done = bf16[128,8,256]{2,1,0:T(8,128)(2,1)} async-done(((bf16[128,8,256]{2,1,0:T(8,128)(2,1)}), bf16[128,8,256]{2,1,0:T(8,128)(2,1)}, u32[]{:S(2)}, u32[]{:S(2)}) %all-to-all-start) | async-done | bytes 524320 | tf_op jit(solution)/shard_map/all_to_all | solution.py:48
  46.1 4.8 %all-to-all-start.2 = ((bf16[8,256,256]{2,1,0:T(8,128)(2,1)}), bf16[8,256,256]{2,1,0:T(8,128)(2,1)S(1)}, u32[]{:S(2)}, u32[]{:S(2)}) async-start(bf16[8,256,256]{2,1,0:T(8,128)(2,1)} %bitcast.46), calls=%async_computation.2 | async-start | bytes 2097152 | tf_op jit(solution)/shard_map/all_to_all | solution.py:53
  51.6 14.4 %all-to-all-done.2 = bf16[8,256,256]{2,1,0:T(8,128)(2,1)S(1)} async-done(((bf16[8,256,256]{2,1,0:T(8,128)(2,1)}), bf16[8,256,256]{2,1,0:T(8,128)(2,1)S(1)}, u32[]{:S(2)}, u32[]{:S(2)}) %all-to-all-start.2) | async-done | bytes 1048608 | tf_op jit(solution)/shard_map/all_to_all | solution.py:53
  66.0 10.3 %pad_maximum_fusion = bf16[6144,256]{1,0:T(8,128)(2,1)} fusion(bf16[2048,256]{1,0:T(8,128)(2,1)S(1)} %bitcast.47, bf16[1024,256]{1,0:T(8,128)(2,1)} %bitcast.5, bf16[3072,256]{1,0:T(8,128)(2,1)S(1)} %copy-done.6), kind=kLoop, calls=%fused_computation.43 | loop fusion | flops 9437184 | bytes 6291456 | tf_op jit(solution)/shard_map/concatenate | solution.py:55
  76.3 1.9 broadcast_in_dim.12
  78.2 30.3 %while.20 = (s32[]{:T(128)}, f32[24,128,256]{2,0,1:T(8,128)}, s32[]{:T(128)}, s32[288]{0:T(512)S(1)}, s32[]{:T(128)}, /*index=5*/bf16[288,128,128]{2,1,0:T(8,128...) while((s32[]{:T(128)}, f32[24,128,256]{2,0,1:T(8,128)}, ...), condition=%wide.region_1.2_spmd, body=%wide.region_0.1_spmd.sunk | while | flops 1712068736 | bytes 78650992 | solution.py:81
  78.4 0.7 compare_convert_fusion.4
  79.0 0.1 compare_select_fusion.6
  79.2 7.9 %gather_fusion = bf16[96,128,256]{2,1,0:T(8,128)(2,1)} fusion(bf16[48,128,256]{2,1,0:T(8,128)(2,1)} %get-tuple-element.264, s32[1024]{0:T(1024)S(1)} %pad_clamp_fusion.5), kind=kCustom, calls=%fused_computation.clone.1 | custom fusion | bytes 12583296 | tf_op jit(solution)/shard_map/while/body/gather | solution.py:72
  87.1 5.7 %fusion.61 = f32[96,128,256]{2,1,0:T(8,128)S(1)} fusion(bf16[96,128,256]{2,1,0:T(8,128)(2,1)} %gather_fusion, bf16[288,128,128]{2,1,0:T(8,128)(2,1)} %get-tuple-element.262, s32[]{:T(128)S(6)} %select_n.56), kind=kOutput, calls=%fused_computation.7.clone.1 | convolution fusion | flops 805306368 | bytes 22020100 | tf_op jit(solution)/shard_map/while/body/tij,tjd->tid/dot_general | solution.py:71
  92.8 13.7 %fusion.62 = f32[24,128,256]{2,0,1:T(8,128)S(1)} fusion(f32[24,128,256]{2,0,1:T(8,128)S(1)} %copy-done.4, f32[96,128,256]{2,1,0:T(8,128)S(1)} %fusion.61, f32[96]{0:T(128)S(1)} %compare_convert_fusion.4, s32[96]{0:T(128)S(1)} %dynamic_slice.32), kind=kOutput, calls=%fused_computation.9.clone.1 | convolution fusion | flops 906760704 | bytes 18875136 | tf_op jit(solution)/shard_map/while/body/tr,tid->rid/dot_general | solution.py:77
  106.5 1.7 copy-done.5
  108.5 2.2 broadcast_multiply_fusion
  110.7 1.0 copy.26
  111.7 0.4 copy-done.8
  112.1 0.4 bitcast_add_fusion
  112.5 0.5 copy-done.12
  113.0 2.3 multiply_convert_fusion
  115.3 0.2 copy-done.10
  115.5 2.9 fusion.31
  118.5 3.5 broadcast_in_dim.13
  122.0 30.3 %while.21 = (s32[]{:T(128)}, f32[48,128,256]{2,0,1:T(8,128)}, s32[]{:T(128)}, s32[288]{0:T(512)S(1)}, s32[]{:T(128)}, /*index=5*/bf16[288,128,128]{2,1,0:T(8,128...) while((s32[]{:T(128)}, f32[48,128,256]{2,0,1:T(8,128)}, ...), condition=%wide.region_3.4_spmd, body=%wide.region_2.3_spmd.sunk | while | flops 2618829312 | bytes 110108272 | solution.py:117
  122.1 0.7 compare_convert_fusion.5
  122.8 0.1 compare_select_fusion.7
  122.9 5.9 %gather_fusion.1 = bf16[96,128,256]{2,1,0:T(8,128)(2,1)} fusion(bf16[24,128,256]{2,1,0:T(8,128)(2,1)S(1)} %get-tuple-element.300, s32[1024]{0:T(1024)S(1)} %pad_clamp_fusion.6), kind=kCustom, calls=%fused_computation.1.clone.1 | custom fusion | bytes 12583296 | tf_op jit(solution)/shard_map/while/body/gather | solution.py:108
  128.9 5.7 %fusion.67 = f32[96,128,256]{2,1,0:T(8,128)S(1)} fusion(bf16[96,128,256]{2,1,0:T(8,128)(2,1)} %gather_fusion.1, bf16[288,128,128]{2,1,0:T(8,128)(2,1)} %get-tuple-element.298, s32[]{:T(128)S(6)} %select_n.58), kind=kOutput, calls=%fused_computation.23.clone.1 | convolution fusion | flops 805306368 | bytes 22020100 | tf_op jit(solution)/shard_map/while/body/tji,tjd->tid/dot_general | solution.py:107
  134.6 14.8 %fusion.68 = f32[48,128,256]{2,0,1:T(8,128)S(1)} fusion(f32[48,128,256]{2,0,1:T(8,128)S(1)} %copy-done.2, f32[96,128,256]{2,1,0:T(8,128)S(1)} %fusion.67, f32[96]{0:T(128)S(1)} %compare_convert_fusion.5, s32[96]{0:T(128)S(1)} %dynamic_slice.35), kind=kOutput, calls=%fused_computation.25.clone.1 | convolution fusion | flops 1813521408 | bytes 25166592 | tf_op jit(solution)/shard_map/while/body/tc,tid->cid/dot_general | solution.py:113
  149.4 2.7 copy-done.3
  152.3 6.2 %copy.29 = bf16[48,128,256]{2,1,0:T(8,128)(2,1)S(1)} copy(f32[48,128,256]{2,0,1:T(8,128)} %get-tuple-element.90) | data formatting | bytes 9437184 | tf_op jit(solution)/shard_map/while | solution.py:117
  158.5 0.8 slice.19
  159.3 123.0 %all-to-all-start.3 = ((bf16[128,8,256]{2,1,0:T(8,128)(2,1)}), bf16[128,8,256]{2,1,0:T(8,128)(2,1)S(1)}, u32[]{:S(2)}, u32[]{:S(2)}) async-start(bf16[128,8,256]{2,1,0:T(8,128)(2,1)} %bitcast.15), calls=%async_computation.3 | async-start | bytes 1048576 | tf_op jit(solution)/shard_map/all_to_all | solution.py:130
  282.4 5.0 %fusion.34 = f32[256,256]{1,0:T(8,128)} fusion(f32[3072,256]{1,0:T(8,128)} %copy-done.7, f32[3072,256]{1,0:T(8,128)} %copy-done.15, bf16[3072,256]{1,0:T(8,128)(2,1)S(1)} %copy-done.11), kind=kOutput, calls=%fused_computation.52 | convolution fusion | flops 411303936 | bytes 8126464 | tf_op jit(solution)/shard_map/dot_general | solution.py:94
  287.4 2.1 slice.7
  289.6 2.6 copy.28
  292.2 139.4 %all-reduce.2.cloned.1.call-done = f32[256,256]{1,0:T(8,128)} async-done(((f32[256,256]{1,0:T(8,128)}), f32[256,256]{1,0:T(8,128)}) %all-reduce.2.cloned.1.call-update) | async-done | bytes 262160 | tf_op jit(solution)/shard_map/psum | solution.py:133
  431.6 1.7 broadcast_multiply_fusion.1
  433.3 9.7 %scatter_custom_fusion = f32[3072,256]{1,0:T(8,128)} fusion(f32[3072,256]{1,0:T(8,128)} %bitcast.48, s32[1024]{0:T(1024)} %bitcast.51, bf16[128,8,256]{2,1,0:T(8,128)(2,1)S(1)} %all-to-all-done.3), kind=kCustom, calls=%fused_computation.50 | custom fusion | flops 524288 | bytes 3670016 | tf_op jit(solution)/shard_map/scatter-add | solution.py:132
  (38 shorter events, 0.3 us)
Async XLA Ops:
  7.2 27.2 %copy-start = (bf16[3072,256]{1,0:T(8,128)(2,1)S(1)}, bf16[3072,256]{1,0:T(8,128)(2,1)}, u32[]{:S(2)}) copy-start(bf16[3072,256]{1,0:T(8,128)(2,1)} %param.17) | copy-start | bytes 4718596
  8.6 14.5 %all-to-all-start.1 = ((s32[8,1,2]{2,1,0:T(1,128)}), s32[8,1,2]{2,1,0:T(1,128)S(1)}, u32[]{:S(2)}, u32[]{:S(2)}) async-start(s32[8,1,2]{2,1,0:T(1,128)} %copy.25), calls=%async_computation.1 | async-start | bytes 8192 | tf_op jit(solution)/shard_map/all_to_all | solution.py:50
  16.4 0.6 copy-start.9
  23.2 42.9 %copy-start.6 = (bf16[3072,256]{1,0:T(8,128)(2,1)S(1)}, bf16[3072,256]{1,0:T(8,128)(2,1)}, u32[]{:S(2)}) copy-start(bf16[3072,256]{1,0:T(8,128)(2,1)} %param.15) | copy-start | bytes 4718596
  23.2 22.9 %all-to-all-start = ((bf16[128,8,256]{2,1,0:T(8,128)(2,1)}), bf16[128,8,256]{2,1,0:T(8,128)(2,1)}, u32[]{:S(2)}, u32[]{:S(2)}) async-start(bf16[128,8,256]{2,1,0:T(8,128)(2,1)} %bitcast.49), calls=%async_computation | async-start | bytes 1048576 | tf_op jit(solution)/shard_map/all_to_all | solution.py:48
  46.1 19.9 %all-to-all-start.2 = ((bf16[8,256,256]{2,1,0:T(8,128)(2,1)}), bf16[8,256,256]{2,1,0:T(8,128)(2,1)S(1)}, u32[]{:S(2)}, u32[]{:S(2)}) async-start(bf16[8,256,256]{2,1,0:T(8,128)(2,1)} %bitcast.46), calls=%async_computation.2 | async-start | bytes 2097152 | tf_op jit(solution)/shard_map/all_to_all | solution.py:53
  76.3 1.9 copy-start.13
  76.3 1.9 copy-start.14
  87.1 5.7 %copy-start.4 = (f32[24,128,256]{2,0,1:T(8,128)S(1)}, f32[24,128,256]{2,0,1:T(8,128)}, u32[]{:S(2)}) copy-start(f32[24,128,256]{2,0,1:T(8,128)} %get-tuple-element.246) | copy-start | bytes 9437188 | tf_op jit(solution)/shard_map/while
  106.5 1.7 copy-start.5
  110.7 1.4 copy-start.8
  112.1 0.9 copy-start.12
  113.0 2.3 copy-start.7
  113.0 2.5 copy-start.10
  115.3 3.2 copy-start.15
  128.9 5.7 %copy-start.2 = (f32[48,128,256]{2,0,1:T(8,128)S(1)}, f32[48,128,256]{2,0,1:T(8,128)}, u32[]{:S(2)}) copy-start(f32[48,128,256]{2,0,1:T(8,128)} %get-tuple-element.282) | copy-start | bytes 18874372 | tf_op jit(solution)/shard_map/while
  149.4 2.7 copy-start.3
  152.2 130.1 %copy-start.11 = (bf16[3072,256]{1,0:T(8,128)(2,1)S(1)}, bf16[3072,256]{1,0:T(8,128)(2,1)}, u32[]{:S(2)}) copy-start(bf16[3072,256]{1,0:T(8,128)(2,1)} %param.18) | copy-start | bytes 4718596
  159.3 273.9 %all-to-all-start.3 = ((bf16[128,8,256]{2,1,0:T(8,128)(2,1)}), bf16[128,8,256]{2,1,0:T(8,128)(2,1)S(1)}, u32[]{:S(2)}, u32[]{:S(2)}) async-start(bf16[128,8,256]{2,1,0:T(8,128)(2,1)} %bitcast.15), calls=%async_computation.3 | async-start | bytes 1048576 | tf_op jit(solution)/shard_map/all_to_all | solution.py:130
  282.3 149.3 %all-reduce.2.cloned.1.call-start = ((), (), s32[]{:S(2)}) async-start(), calls=%async_computation.4 | async-start | bytes 524288 | tf_op jit(solution)/shard_map/psum | solution.py:133
  289.5 153.5 %copy-start.1 = (bf16[3072,256]{1,0:T(8,128)(2,1)S(1)}, bf16[3072,256]{1,0:T(8,128)(2,1)}, u32[]{:S(2)}) copy-start(bf16[3072,256]{1,0:T(8,128)(2,1)} %param.17) | copy-start | bytes 4718596
Sparse Core Ops, SparseCore 0:
  288.5 143.0 all-reduce.1
where the time goes:
time: 456 us; the launch traced here: 450 us
  waiting for transfers between devices  164 us (36%)
  starting transfers between devices  145 us (32%)
  matrix products  50.1 us (11%)
  local copies, waits for them, and re-layouts  48.9 us (11%)
  other arithmetic  26.4 us (6%)
  between operations  15.1 us (3%)
    psum x1, waiting for transfers between devices, per_device(): weight_total = lax.psum(weight_part, ('dom', 'grp'))  139 us
    all_to_all x1, starting transfers between devices, per_device(): lax.all_to_all(fresh_grads, ('dom', 'grp'), split_axis=0, concat_axis=0,...  123 us
    dot_general x1, matrix products, backward_turn(): jnp.einsum('tc,tid->cid', onto_mask, spread, precision=lax.Precision.HIGH...  14.8 us
    all_to_all x1, waiting for transfers between devices, per_device(): lax.all_to_all(served, 'dom', split_axis=0, concat_axis=0, tiled=True)  14.4 us
    dot_general x1, matrix products, forward_turn(): jnp.einsum('tr,tid->rid', placing, products, precision=lax.Precision.HIGH...  13.7 us
    concatenate x1, other arithmetic, per_device(): columns = jnp.concatenate([inputs, arrived, cached], axis=0)  10.3 us
    all_to_all x1, waiting for transfers between devices, per_device(): lax.all_to_all(outgoing, ('dom', 'grp'), split_axis=0, concat_axis=0, til...  10.1 us
    all_to_all x1, starting transfers between devices, per_device(): lax.all_to_all(outgoing, ('dom', 'grp'), split_axis=0, concat_axis=0, til...  9.95 us
  transfers between devices with their start and end apart: 5, of which 3 were waited for; matrix products, arithmetic and copies ran while one was open for 5% of the time, Pallas kernels for 0%

commit v1 on v0

--- a/solution.py
+++ b/solution.py
@@ -1,3 +1,4 @@
+import functools
 import math
 import jax
 import jax.numpy as jnp
@@ -6,6 +7,13 @@
 
 alpha_res = 0.1
 beta_map = 0.4
+
+
+def assign_things(my_tile, which_axis):
+    return jnp.sum(lax.all_gather(my_tile, which_axis), 0)
+
+
+proceed_lane_by_axis = functools.partial(assign_things, which_axis=("dom", "grp"))
 
 
 def silu_slope(pre_act):
@@ -130,7 +138,7 @@
     returned = lax.all_to_all(fresh_grads, ("dom", "grp"), split_axis=0, concat_axis=0, tiled=True)
     returned = returned.reshape(peer_count * per_peer, feature_dim).astype(jnp.float32)
     grad_inputs = own_grads.at[send_list.reshape(-1)].add(returned)
-    weight_total = lax.psum(weight_part, ("dom", "grp"))
+    weight_total = proceed_lane_by_axis(weight_part)
     grad_weight = weight_total * (beta_map / math.sqrt(row_count * peer_count))
     return (layer_out, grad_inputs, grad_weight)
 

time: 456 us -> 338 us (0.74)
  waiting for transfers between devices: 164 us -> 33.2 us
  other arithmetic: 26.4 us -> 37.6 us
    psum x1 -> x0, waiting for transfers between devices: 139 us -> none  [per_device(): weight_total = lax.psum(weight_part, ('dom', 'grp'))]
    reduce_sum x0 -> x1, other arithmetic: none -> 12.1 us  [assign_things(): return jnp.sum(lax.all_gather(my_tile, which_axis), 0)]
    all_to_all x1, waiting for transfers between devices: 0.01 us -> 8.59 us  [per_device(): lax.all_to_all(fresh_grads, ('dom', 'grp'), split_axis=0, concat_axis=0,...]
  transfers between devices with their start and end apart: 5 -> 5, of which waited for: 3 -> 3; matrix products, arithmetic and copies ran while one was open for 5% -> 20% of each run, Pallas kernels for 0% -> 0%
where the time goes in v1:
time: 338 us; the launch traced here: 332 us
  starting transfers between devices  145 us (43%)
  local copies, waits for them, and re-layouts  50.2 us (15%)
  matrix products  49.9 us (15%)
  other arithmetic  37.6 us (11%)
  waiting for transfers between devices  33.2 us (10%)
  between operations  15 us (4%)
    all_to_all x1, starting transfers between devices, per_device(): lax.all_to_all(fresh_grads, ('dom', 'grp'), split_axis=0, concat_axis=0,...  124 us
    dot_general x1, matrix products, backward_turn(): jnp.einsum('tc,tid->cid', onto_mask, spread, precision=lax.Precision.HIGH...  14.8 us
    all_to_all x1, waiting for transfers between devices, per_device(): lax.all_to_all(served, 'dom', split_axis=0, concat_axis=0, tiled=True)  14.4 us
    dot_general x1, matrix products, forward_turn(): jnp.einsum('tr,tid->rid', placing, products, precision=lax.Precision.HIGH...  13.7 us
    reduce_sum x1, other arithmetic, assign_things(): return jnp.sum(lax.all_gather(my_tile, which_axis), 0)  12.1 us
    concatenate x1, other arithmetic, per_device(): columns = jnp.concatenate([inputs, arrived, cached], axis=0)  10.3 us
    all_to_all x1, waiting for transfers between devices, per_device(): lax.all_to_all(outgoing, ('dom', 'grp'), split_axis=0, concat_axis=0, til...  10.1 us
    all_to_all x1, starting transfers between devices, per_device(): lax.all_to_all(outgoing, ('dom', 'grp'), split_axis=0, concat_axis=0, til...  9.95 us
  transfers between devices with their start and end apart: 5, of which 3 were waited for; matrix products, arithmetic and copies ran while one was open for 20% of the time, Pallas kernels for 0%

profile of v1, /device:TPU:1, one launch (start us, length us, event | category | flops | bytes accessed | tf_op | source)
XLA Modules:
  0.0 332.2 jit_solution(13790550390070972307)
XLA Ops:
  7.2 1.5 copy.25
  8.6 6.8 %all-to-all-start.1 = ((s32[8,1,2]{2,1,0:T(1,128)}), s32[8,1,2]{2,1,0:T(1,128)S(1)}, u32[]{:S(2)}, u32[]{:S(2)}) async-start(s32[8,1,2]{2,1,0:T(1,128)} %copy.25), calls=%async_computation.1 | async-start | bytes 8192 | tf_op jit(solution)/shard_map/all_to_all | solution.py:58
  15.5 0.8 copy.24
  16.2 0.1 reshape_reshape.4
  16.4 0.6 copy-done.7
  17.0 6.2 %gather_fusion.2 = bf16[1024,256]{1,0:T(8,128)(2,1)} fusion(bf16[3072,256]{1,0:T(8,128)(2,1)} %param.15, s32[1024]{0:T(1024)S(1)} %broadcast_clamp_fusion), kind=kCustom, calls=%fused_computation.2 | custom fusion | bytes 1052672 | tf_op jit(solution)/shard_map/gather | solution.py:55
  23.2 9.9 %all-to-all-start = ((bf16[128,8,256]{2,1,0:T(8,128)(2,1)}), bf16[128,8,256]{2,1,0:T(8,128)(2,1)}, u32[]{:S(2)}, u32[]{:S(2)}) async-start(bf16[128,8,256]{2,1,0:T(8,128)(2,1)} %bitcast.53), calls=%async_computation | async-start | bytes 1048576 | tf_op jit(solution)/shard_map/all_to_all | solution.py:56
  33.1 0.5 broadcast.141
  33.7 0.7 reduce.3
  34.3 0.1 reshape.119
  34.4 1.6 gather_fusion.3
  36.0 10.1 %all-to-all-done = bf16[128,8,256]{2,1,0:T(8,128)(2,1)} async-done(((bf16[128,8,256]{2,1,0:T(8,128)(2,1)}), bf16[128,8,256]{2,1,0:T(8,128)(2,1)}, u32[]{:S(2)}, u32[]{:S(2)}) %all-to-all-start) | async-done | bytes 524320 | tf_op jit(solution)/shard_map/all_to_all | solution.py:56
  46.1 4.8 %all-to-all-start.2 = ((bf16[8,256,256]{2,1,0:T(8,128)(2,1)}), bf16[8,256,256]{2,1,0:T(8,128)(2,1)S(1)}, u32[]{:S(2)}, u32[]{:S(2)}) async-start(bf16[8,256,256]{2,1,0:T(8,128)(2,1)} %bitcast.50), calls=%async_computation.2 | async-start | bytes 2097152 | tf_op jit(solution)/shard_map/all_to_all | solution.py:61
  51.6 14.4 %all-to-all-done.2 = bf16[8,256,256]{2,1,0:T(8,128)(2,1)S(1)} async-done(((bf16[8,256,256]{2,1,0:T(8,128)(2,1)}), bf16[8,256,256]{2,1,0:T(8,128)(2,1)S(1)}, u32[]{:S(2)}, u32[]{:S(2)}) %all-to-all-start.2) | async-done | bytes 1048608 | tf_op jit(solution)/shard_map/all_to_all | solution.py:61
  66.0 10.3 %pad_maximum_fusion = bf16[6144,256]{1,0:T(8,128)(2,1)} fusion(bf16[2048,256]{1,0:T(8,128)(2,1)S(1)} %bitcast.51, bf16[1024,256]{1,0:T(8,128)(2,1)} %bitcast.5, bf16[3072,256]{1,0:T(8,128)(2,1)S(1)} %copy-done.5), kind=kLoop, calls=%fused_computation.43 | loop fusion | flops 9437184 | bytes 6291456 | tf_op jit(solution)/shard_map/concatenate | solution.py:63
  76.3 1.9 broadcast_in_dim.12
  78.2 30.3 %while.20 = (s32[]{:T(128)}, f32[24,128,256]{2,0,1:T(8,128)}, s32[]{:T(128)}, s32[288]{0:T(512)S(1)}, s32[]{:T(128)}, /*index=5*/bf16[288,128,128]{2,1,0:T(8,128...) while((s32[]{:T(128)}, f32[24,128,256]{2,0,1:T(8,128)}, ...), condition=%wide.region_1.2_spmd, body=%wide.region_0.1_spmd.sunk | while | flops 1712068736 | bytes 78651000 | solution.py:89
  78.5 7.9 %gather_fusion = bf16[96,128,256]{2,1,0:T(8,128)(2,1)} fusion(bf16[48,128,256]{2,1,0:T(8,128)(2,1)} %get-tuple-element.264, s32[1024]{0:T(1024)S(1)} %pad_clamp_fusion.5), kind=kCustom, calls=%fused_computation.clone.1 | custom fusion | bytes 12583296 | tf_op jit(solution)/shard_map/while/body/gather | solution.py:80
  86.4 5.7 %fusion.61 = f32[96,128,256]{2,1,0:T(8,128)S(1)} fusion(bf16[96,128,256]{2,1,0:T(8,128)(2,1)} %gather_fusion, bf16[288,128,128]{2,1,0:T(8,128)(2,1)} %get-tuple-element.262, s32[]{:T(128)S(6)} %select_n.56), kind=kOutput, calls=%fused_computation.7.clone.1 | convolution fusion | flops 805306368 | bytes 22020100 | tf_op jit(solution)/shard_map/while/body/tij,tjd->tid/dot_general | solution.py:79
  92.0 0.7 compare_convert_fusion.4
  92.7 0.1 dynamic_slice.32
  92.8 13.7 %fusion.62 = f32[24,128,256]{2,0,1:T(8,128)S(1)} fusion(f32[24,128,256]{2,0,1:T(8,128)S(1)} %copy-done.3, f32[96,128,256]{2,1,0:T(8,128)S(1)} %fusion.61, f32[96]{0:T(128)S(1)} %compare_convert_fusion.4, s32[96]{0:T(128)S(1)} %dynamic_slice.32), kind=kOutput, calls=%fused_computation.9.clone.1 | convolution fusion | flops 906760704 | bytes 18875136 | tf_op jit(solution)/shard_map/while/body/tr,tid->rid/dot_general | solution.py:85
  106.5 1.7 copy-done.4
  108.5 2.2 broadcast_multiply_fusion
  110.7 1.0 copy.26
  111.7 0.4 copy-done.6
  112.1 0.4 bitcast_add_fusion
  112.5 0.5 copy-done.9
  113.0 2.3 multiply_convert_fusion
  115.3 1.7 copy-done.12
  117.0 2.2 fusion.34
  119.2 5.6 %fusion.31 = bf16[3072,256]{1,0:T(8,128)(2,1)S(1)} fusion(bf16[256,256]{1,0:T(8,128)(2,1)S(1)} %copy-done.9, f32[3072,256]{1,0:T(8,128)} %copy-done.12, bf16[3072,256]{1,0:T(8,128)(2,1)S(1)} %copy-done.8), kind=kOutput, calls=%fused_computation.42 | convolution fusion | flops 421527552 | bytes 6422528 | tf_op jit(solution)/shard_map/dot_general | solution.py:105
  124.8 3.4 %broadcast_in_dim.13 = f32[48,128,256]{2,0,1:T(8,128)} broadcast(f32[]{:T(128)} %constant.39.clone.1), dimensions={} | broadcast | bytes 6291460 | tf_op jit(solution)/shard_map/broadcast_in_dim | solution.py:129
  128.3 30.2 %while.21 = (s32[]{:T(128)}, f32[48,128,256]{2,0,1:T(8,128)}, s32[]{:T(128)}, s32[288]{0:T(512)S(1)}, s32[]{:T(128)}, /*index=5*/bf16[288,128,128]{2,1,0:T(8,128...) while((s32[]{:T(128)}, f32[48,128,256]{2,0,1:T(8,128)}, ...), condition=%wide.region_3.4_spmd, body=%wide.region_2.3_spmd.sunk | while | flops 2618829312 | bytes 103816832 | solution.py:125
  128.5 5.9 %gather_fusion.1 = bf16[96,128,256]{2,1,0:T(8,128)(2,1)} fusion(bf16[24,128,256]{2,1,0:T(8,128)(2,1)S(1)} %get-tuple-element.300, s32[1024]{0:T(1024)S(1)} %pad_clamp_fusion.6), kind=kCustom, calls=%fused_computation.1.clone.1 | custom fusion | bytes 12583296 | tf_op jit(solution)/shard_map/while/body/gather | solution.py:116
  134.4 5.7 %fusion.67 = f32[96,128,256]{2,1,0:T(8,128)S(1)} fusion(bf16[96,128,256]{2,1,0:T(8,128)(2,1)} %gather_fusion.1, bf16[288,128,128]{2,1,0:T(8,128)(2,1)} %get-tuple-element.298, s32[]{:T(128)S(6)} %select_n.58), kind=kOutput, calls=%fused_computation.23.clone.1 | convolution fusion | flops 805306368 | bytes 22020100 | tf_op jit(solution)/shard_map/while/body/tji,tjd->tid/dot_general | solution.py:115
  140.2 0.7 compare_convert_fusion.5
  140.9 14.8 %fusion.68 = f32[48,128,256]{2,0,1:T(8,128)S(1)} fusion(f32[48,128,256]{2,0,1:T(8,128)S(1)} %bitcast.48, f32[96,128,256]{2,1,0:T(8,128)S(1)} %fusion.67, f32[96]{0:T(128)S(1)} %compare_convert_fusion.5, s32[96]{0:T(128)S(1)} %dynamic_slice.35), kind=kOutput, calls=%fused_computation.25.clone.1 | convolution fusion | flops 1813521408 | bytes 25166592 | tf_op jit(solution)/shard_map/while/body/tc,tid->cid/dot_general | solution.py:121
  155.7 2.6 copy-done.2
  158.5 6.1 %copy.29 = bf16[48,128,256]{2,1,0:T(8,128)(2,1)S(1)} copy(f32[48,128,256]{2,0,1:T(8,128)} %get-tuple-element.90) | data formatting | bytes 9437184 | tf_op jit(solution)/shard_map/while | solution.py:125
  164.6 0.9 slice.19
  165.5 123.8 %all-to-all-start.3 = ((bf16[128,8,256]{2,1,0:T(8,128)(2,1)}), bf16[128,8,256]{2,1,0:T(8,128)(2,1)S(1)}, u32[]{:S(2)}, u32[]{:S(2)}) async-start(bf16[128,8,256]{2,1,0:T(8,128)(2,1)} %bitcast.15), calls=%async_computation.3 | async-start | bytes 1048576 | tf_op jit(solution)/shard_map/all_to_all | solution.py:138
  289.3 2.1 slice.7
  291.4 2.6 copy.28
  294.0 8.6 %all-to-all-done.3 = bf16[128,8,256]{2,1,0:T(8,128)(2,1)S(1)} async-done(((bf16[128,8,256]{2,1,0:T(8,128)(2,1)}), bf16[128,8,256]{2,1,0:T(8,128)(2,1)S(1)}, u32[]{:S(2)}, u32[]{:S(2)}) %all-to-all-start.3) | async-done | bytes 524320 | tf_op jit(solution)/shard_map/all_to_all | solution.py:138
  302.6 9.7 %scatter_custom_fusion = f32[3072,256]{1,0:T(8,128)} fusion(f32[3072,256]{1,0:T(8,128)} %bitcast.52, s32[1024]{0:T(1024)} %bitcast.55, bf16[128,8,256]{2,1,0:T(8,128)(2,1)S(1)} %all-to-all-done.3), kind=kCustom, calls=%fused_computation.50 | custom fusion | flops 524288 | bytes 3670016 | tf_op jit(solution)/shard_map/scatter-add | solution.py:140
  312.4 12.1 %reduce_sum.9 = f32[256,256]{1,0:T(8,128)S(1)} reduce(f32[128,256,256]{2,1,0:T(8,128)} %bitcast.49, f32[]{:T(128)} %constant.39.clone.1), dimensions={0}, to_apply=%region_5.6 | reduce | flops 8323072 | bytes 33816580 | tf_op jit(solution)/shard_map/reduce_sum | solution.py:13
  324.4 0.7 broadcast_multiply_fusion.1
  (38 shorter events, 0.4 us)
Async XLA Ops:
  7.2 27.3 %copy-start = (bf16[3072,256]{1,0:T(8,128)(2,1)S(1)}, bf16[3072,256]{1,0:T(8,128)(2,1)}, u32[]{:S(2)}) copy-start(bf16[3072,256]{1,0:T(8,128)(2,1)} %param.17) | copy-start | bytes 4718596
  8.6 14.5 %all-to-all-start.1 = ((s32[8,1,2]{2,1,0:T(1,128)}), s32[8,1,2]{2,1,0:T(1,128)S(1)}, u32[]{:S(2)}, u32[]{:S(2)}) async-start(s32[8,1,2]{2,1,0:T(1,128)} %copy.25), calls=%async_computation.1 | async-start | bytes 8192 | tf_op jit(solution)/shard_map/all_to_all | solution.py:58
  16.4 0.6 copy-start.7
  23.2 42.9 %copy-start.5 = (bf16[3072,256]{1,0:T(8,128)(2,1)S(1)}, bf16[3072,256]{1,0:T(8,128)(2,1)}, u32[]{:S(2)}) copy-start(bf16[3072,256]{1,0:T(8,128)(2,1)} %param.15) | copy-start | bytes 4718596
  23.2 22.9 %all-to-all-start = ((bf16[128,8,256]{2,1,0:T(8,128)(2,1)}), bf16[128,8,256]{2,1,0:T(8,128)(2,1)}, u32[]{:S(2)}, u32[]{:S(2)}) async-start(bf16[128,8,256]{2,1,0:T(8,128)(2,1)} %bitcast.53), calls=%async_computation | async-start | bytes 1048576 | tf_op jit(solution)/shard_map/all_to_all | solution.py:56
  46.1 19.9 %all-to-all-start.2 = ((bf16[8,256,256]{2,1,0:T(8,128)(2,1)}), bf16[8,256,256]{2,1,0:T(8,128)(2,1)S(1)}, u32[]{:S(2)}, u32[]{:S(2)}) async-start(bf16[8,256,256]{2,1,0:T(8,128)(2,1)} %bitcast.50), calls=%async_computation.2 | async-start | bytes 2097152 | tf_op jit(solution)/shard_map/all_to_all | solution.py:61
  50.9 261.4 %all-gather.3.cloned.1.call-start = ((), (), s32[]{:S(2)}) async-start(), calls=%async_computation.4 | async-start | bytes 33816576 | tf_op jit(solution)/shard_map/all_gather | solution.py:13
  76.3 1.9 copy-start.10
  76.3 1.9 copy-start.11
  86.4 6.4 %copy-start.3 = (f32[24,128,256]{2,0,1:T(8,128)S(1)}, f32[24,128,256]{2,0,1:T(8,128)}, u32[]{:S(2)}) copy-start(f32[24,128,256]{2,0,1:T(8,128)} %get-tuple-element.246) | copy-start | bytes 9437188 | tf_op jit(solution)/shard_map/while
  106.4 1.7 copy-start.4
  110.7 1.4 copy-start.6
  112.1 0.9 copy-start.9
  113.0 4.0 %copy-start.8 = (bf16[3072,256]{1,0:T(8,128)(2,1)S(1)}, bf16[3072,256]{1,0:T(8,128)(2,1)}, u32[]{:S(2)}) copy-start(bf16[3072,256]{1,0:T(8,128)(2,1)} %param.18) | copy-start | bytes 4718596
  115.3 1.7 copy-start.12
  134.4 6.5 %slice-start = ((s8[6291456]{0:T(1024)(128)(4,1)}), s8[4194304]{0:T(1024)(128)(4,1)S(1)}, s32[]{:S(2)}) async-start(s8[6291456]{0:T(1024)(128)(4,1)} %bitcast.47), calls=%async_computation.5 | async-start | bytes 8388608 | tf_op jit(solution)/shard_map/while
  134.4 6.5 %slice-start.1 = ((s8[6291456]{0:T(1024)(128)(4,1)}), s8[2097152]{0:T(1024)(128)(4,1)S(1)}, s32[]{:S(2)}) async-start(s8[6291456]{0:T(1024)(128)(4,1)} %bitcast.47), calls=%async_computation.6 | async-start | bytes 4194304 | tf_op jit(solution)/shard_map/while
  155.7 2.6 copy-start.2
  165.5 137.1 %all-to-all-start.3 = ((bf16[128,8,256]{2,1,0:T(8,128)(2,1)}), bf16[128,8,256]{2,1,0:T(8,128)(2,1)S(1)}, u32[]{:S(2)}, u32[]{:S(2)}) async-start(bf16[128,8,256]{2,1,0:T(8,128)(2,1)} %bitcast.15), calls=%async_computation.3 | async-start | bytes 1048576 | tf_op jit(solution)/shard_map/all_to_all | solution.py:138
  312.4 12.8 %copy-start.1 = (bf16[3072,256]{1,0:T(8,128)(2,1)S(1)}, bf16[3072,256]{1,0:T(8,128)(2,1)}, u32[]{:S(2)}) copy-start(bf16[3072,256]{1,0:T(8,128)(2,1)} %param.17) | copy-start | bytes 4718596
Sparse Core Ops, SparseCore 0:
  119.3 161.9 all-gather.2
